TPU v7x, 128 devices: a whole 4x4x4 slice. The times are simulated.
128 devices in a mesh: tm: 64 (over z, y, x), tile: 2 (over core).
Axes of the slice: x: 4, y: 4, z: 4, core: 2. Of those that a mesh axis runs over, the one named last changes fastest.
Arguments:
- prior_space: float32 [1536, 1536], P('tile'), as said below
- node_gain: float32 [1536], replicated, may hold values from 0.4 to 1
- time_diag: float32 [128], P('tm'), may hold values from 0.6 to 1.5
- rho: float32 [128], P('tm'), may hold values from 0.2 to 0.95
- obs_values: float32 [2, 8192, 16, 768], P('tile', 'tm'), may hold values from -0.5 to 0.5
- obs_weight: float32 [2, 8192, 16], P('tile', 'tm'), may hold values from 0.25 to 4
- obs_step: int32 [2, 64, 128], P('tile', 'tm'), may hold values from 0 to 127, each once within a row
Outputs:
- separator_block: float32 [64, 1536, 1536], P('tm', 'tile')
- separator_coupling: float32 [64, 1536, 1536], P('tm', 'tile')
- interior_logdet: float32 [64], P('tm')
Inputs may be any that keep to these rules, and one draw needn't show every extreme that they name: prior_space is symmetric and each diagonal entry exceeds the sum of magnitudes of the other entries of its row. For each node block c and each index m of tm, obs_step[c, m] names every time step exactly once.
All inputs are finite; a program needn't handle non-finite values.
Results may differ from a plain program's by a relative error of at most 0.00013.
Values sent between devices are 32-bit elements; how exact they have to be, the bound alone decides.
No kernel may reach another device: no remote copies, remote signals or barrier semaphores. Data moves between devices by JAX's collectives and lax.ppermute only.
A program may use at most 192 MiB of HBM per device.

v0:
```python
import jax
import jax.numpy as jnp
from jax import lax
from jax.sharding import PartitionSpec as P


def from_root(shard, axis, root):
    return lax.dynamic_index_in_dim(lax.all_gather(shard, axis), root, 0, keepdims=False)


def from_everyone(shard, axis):
    copies = jnp.broadcast_to(shard, (lax.axis_size(axis), *shard.shape))
    return lax.all_to_all(copies, axis, split_axis=0, concat_axis=0, tiled=True)


def of_everyone(shard, axis):
    everything = from_everyone(shard, axis)
    return jnp.sum(everything, axis=0)


def from_behind(block, axis, distance):
    devices = range(lax.axis_size(axis))
    route = [(i - distance, i) for i in devices if i - distance in devices]
    return lax.ppermute(block, axis, route)


def gram_of(exchanged):
    tile_values, tile_weights = exchanged
    weighted = tile_values * tile_weights[..., None]
    return jnp.einsum("skrb,skrc->kbc", weighted, tile_values, precision=lax.Precision.HIGHEST)


def on_device(prior_space, node_gain, time_diag, rho, obs_values, obs_weight, obs_step):
    precise = lax.Precision.HIGHEST
    rows_of_block = prior_space.shape[0]
    node_count = prior_space.shape[1]
    count_of_tiles = lax.axis_size("tile")
    part_count = lax.axis_size("tm")
    index_of_tile = lax.axis_index("tile")
    row_start = index_of_tile * rows_of_block
    tile_values = obs_values[0]
    tile_weights = obs_weight[0]
    tile_steps = obs_step[0, 0]
    tile_total = tile_steps.shape[0]
    obs_rows = tile_values.shape[1]
    send_values = (
        jnp.zeros((tile_total, obs_rows, rows_of_block), jnp.float32)
        .at[tile_steps]
        .set(tile_values)
    )
    send_weights = jnp.zeros((tile_total, obs_rows), jnp.float32).at[tile_steps].set(tile_weights)
    send_values = send_values.reshape(part_count, 2, obs_rows, rows_of_block)
    send_weights = send_weights.reshape(part_count, 2, obs_rows)
    obs_grams = gram_of(
        (
            lax.all_to_all(send_values, "tm", split_axis=0, concat_axis=0, tiled=True),
            lax.all_to_all(send_weights, "tm", split_axis=0, concat_axis=0, tiled=True),
        )
    )

    def assemble(coef, gram_step):
        scaled_rows = coef * prior_space
        diag_part = lax.dynamic_slice_in_dim(scaled_rows, row_start, rows_of_block, 1) + gram_step
        return lax.dynamic_update_slice_in_dim(scaled_rows, diag_part, row_start, 1)

    interior = assemble(time_diag[0], obs_grams[0])
    separator = assemble(time_diag[1], obs_grams[1])
    own_gain = lax.dynamic_slice_in_dim(node_gain, row_start, rows_of_block)
    gain_tile = jnp.eye(rows_of_block, dtype=jnp.float32) * own_gain[None, :]
    trailing_matrix = interior
    schur_rows = jnp.zeros((rows_of_block, node_count), jnp.float32)
    log_total = jnp.zeros((), jnp.float32)
    for elimination_round in range(count_of_tiles):
        diag_tile = lax.dynamic_slice_in_dim(trailing_matrix, row_start, rows_of_block, 1)
        lower_factor = jnp.linalg.cholesky(diag_tile)
        seeded = lax.dynamic_update_slice_in_dim(trailing_matrix, gain_tile, row_start, 1)
        rows_solved = lax.linalg.triangular_solve(lower_factor, seeded, left_side=True, lower=True)
        log_total = log_total + jnp.where(
            index_of_tile == elimination_round,
            2.0 * jnp.sum(jnp.log(jnp.diagonal(lower_factor))),
            0.0,
        )
        rows_of_panel = from_root(rows_solved, "tile", elimination_round)
        boundary_column = (elimination_round + 1) * rows_of_block
        coupling_transposed = lax.dynamic_slice_in_dim(rows_of_panel, row_start, rows_of_block, 1)
        cleared_panel = trailing_matrix.at[
            :, elimination_round * rows_of_block : boundary_column
        ].set(0.0)
        updated_block = cleared_panel - jnp.dot(
            coupling_transposed.T, rows_of_panel, precision=precise
        )
        trailing_matrix = jnp.where(
            index_of_tile > elimination_round, updated_block, trailing_matrix
        )
        local_columns = jnp.where(index_of_tile <= elimination_round, coupling_transposed, 0.0)
        schur_rows = schur_rows.at[:, :boundary_column].add(
            jnp.dot(local_columns.T, rows_of_panel[:, :boundary_column], precision=precise)
        )
    log_all = of_everyone(log_total, "tile")
    interior_logdet = (log_all / node_count).reshape(1)
    incoming = from_behind(rho[0] * rho[0] * schur_rows, "tm", -1)
    separator_block = separator - rho[1] * rho[1] * schur_rows - incoming
    separator_coupling = -(rho[0] * rho[1]) * schur_rows
    return (separator_block[None], separator_coupling[None], interior_logdet)


def solution(mesh):
    in_specs = (
        P("tile", None),
        P(),
        P("tm"),
        P("tm"),
        P("tile", "tm", None, None),
        P("tile", "tm", None),
        P("tile", "tm", None),
    )
    out_specs = (P("tm", "tile", None), P("tm", "tile", None), P("tm"))
    return jax.shard_map(
        on_device, mesh=mesh, in_specs=in_specs, out_specs=out_specs, check_vma=False
    )
```

profile of v0, /device:TPU:30, one launch (start us, length us, event | category | flops | bytes accessed | tf_op | source)
XLA Modules:
  0.0 953.4 jit_solution(16753631129663737262)
XLA Ops:
  24.6 21.5 %scatter_fusion = f32[128,16,768]{2,1,0:T(8,128)} fusion(f32[128,16,768]{2,1,0:T(8,128)} %broadcast_in_dim.33, s32[128]{0:T(128)S(1)} %fusion.135, f32[128,16,768]{2,1,0:T(8,128)} %bitcast.194), kind=kCustom, calls=%fused_computation.2 | custom fusion | bytes 18874880 | tf_op jit(solution)/shard_map/scatter | solution.py:49
  72.4 65.1 %all-to-all-done = f32[64,2,16,768]{3,2,1,0:T(8,128)} async-done(((f32[64,2,16,768]{3,2,1,0:T(8,128)}), f32[64,2,16,768]{3,2,1,0:T(8,128)}, u32[]{:S(2)}, u32[]{:S(2)}) %all-to-all-start) | async-done | bytes 6291488 | tf_op jit(solution)/shard_map/all_to_all | solution.py:56
  137.6 20.7 %fusion.50 = f32[2,768,768]{1,2,0:T(8,128)S(1)} fusion(f32[64,2,16,768]{3,2,1,0:T(8,128)} %all-to-all-done, f32[64,2,16]{2,1,0:T(2,128)S(1)} %all-to-all-done.1), kind=kOutput, calls=%fused_computation.81 | convolution fusion | flops 14497087488 | bytes 11018240 | tf_op jit(solution)/shard_map/skrb,skrc->kbc/dot_general | solution.py:30
  176.9 11.7 %cholesky.453 = f32[128,128]{1,0:T(8,128)S(1)} custom-call(f32[128,128]{1,0:T(8,128)S(1)} %cholesky.669), custom_call_target="Cholesky" | custom-call | tf_op jit(solution)/shard_map/jit(cholesky)/cholesky | solution.py:75
  201.4 11.7 %cholesky.472 = f32[128,128]{1,0:T(8,128)S(1)} custom-call(f32[128,128]{1,0:T(8,128)S(1)} %cholesky.673), custom_call_target="Cholesky" | custom-call | tf_op jit(solution)/shard_map/jit(cholesky)/cholesky | solution.py:75
  225.1 11.7 %cholesky.493 = f32[128,128]{1,0:T(8,128)S(1)} custom-call(f32[128,128]{1,0:T(8,128)S(1)} %cholesky.678), custom_call_target="Cholesky" | custom-call | tf_op jit(solution)/shard_map/jit(cholesky)/cholesky | solution.py:75
  249.2 12.1 %cholesky.512 = f32[128,128]{1,0:T(8,128)S(1)} custom-call(f32[128,128]{1,0:T(8,128)S(1)} %cholesky.683), custom_call_target="Cholesky" | custom-call | tf_op jit(solution)/shard_map/jit(cholesky)/cholesky | solution.py:75
  273.6 11.7 %cholesky.531 = f32[128,128]{1,0:T(8,128)S(1)} custom-call(f32[128,128]{1,0:T(8,128)S(1)} %cholesky.688), custom_call_target="Cholesky" | custom-call | tf_op jit(solution)/shard_map/jit(cholesky)/cholesky | solution.py:75
  297.4 11.9 %cholesky.548 = f32[128,128]{1,0:T(8,128)S(1)} custom-call(f32[128,128]{1,0:T(8,128)S(1)} %convolution_subtract_fusion.17), custom_call_target="Cholesky" | custom-call | tf_op jit(solution)/shard_map/jit(cholesky)/cholesky | solution.py:75
  317.1 17.3 %while.8 = (s32[]{:T(128)}, f32[768,768]{1,0:T(8,128)}, s32[6,2]{0,1:T(2,128)S(1)}, f32[6,128,128]{2,1,0:T(8,128)S(1)}, s32[]{:T(128)}) while((s32[]{:T(128)}, f32[768,768]{1,0:T(8,128)}, s32[6,2]{0,1:T(2,128)S(1)}, f32[6,128,128]{2,1,0:T(8,128)S(1)}, s32[]{:T(128)}) %tuple.102), condition=%wide.while_cond.3, body=%wide.while_body.3.sunk | while | flops 2 | bytes 131189 | solution.py:77
  334.4 59.0 %custom-call.50 = f32[6,128,128]{1,2,0:T(8,128)S(1)} custom-call(f32[6,128,128]{2,1,0:T(8,128)S(1)} %get-tuple-element.63), custom_call_target="InvertDiagBlocksLowerTriangular" | custom-call | tf_op jit(solution)/shard_map/triangular_solve/custom-call.5 | solution.py:77
  449.2 27.0 %all-gather.5.cloned.1.call-done = f32[1536,1536]{0,1:T(8,128)} async-done(((f32[768,1536]{0,1:T(8,128)}), f32[1536,1536]{0,1:T(8,128)}) %all-gather.5.cloned.1.call-update) | async-done | bytes 9437200 | tf_op jit(solution)/shard_map/all_gather | solution.py:8
  478.9 15.9 %subtract_select_fusion = f32[768,1536]{0,1:T(8,128)S(1)} fusion(f32[768,1536]{0,1:T(8,128)} %copy-done.1, f32[768,1536]{0,1:T(8,128)} %get-tuple-element.112, f32[768,1536]{0,1:T(8,128)S(1)} %slice.317, pred[]{:T(512)S(6)} %gt.3, s32[]{:T(128)S(6)} %select_n.68), kind=kOutput, calls=%fused_computation.12 | convolution fusion | flops 10873995264 | bytes 21233668 | tf_op jit(solution)/shard_map/dot_general | solution.py:89
  528.0 11.7 %cholesky.582 = f32[128,128]{1,0:T(8,128)S(1)} custom-call(f32[128,128]{1,0:T(8,128)S(1)} %cholesky.696), custom_call_target="Cholesky" | custom-call | tf_op jit(solution)/shard_map/jit(cholesky)/cholesky | solution.py:75
  552.5 11.7 %cholesky.603 = f32[128,128]{1,0:T(8,128)S(1)} custom-call(f32[128,128]{1,0:T(8,128)S(1)} %cholesky.701), custom_call_target="Cholesky" | custom-call | tf_op jit(solution)/shard_map/jit(cholesky)/cholesky | solution.py:75
  576.6 11.8 %cholesky.622 = f32[128,128]{1,0:T(8,128)S(1)} custom-call(f32[128,128]{1,0:T(8,128)S(1)} %cholesky.706), custom_call_target="Cholesky" | custom-call | tf_op jit(solution)/shard_map/jit(cholesky)/cholesky | solution.py:75
  600.8 11.7 %cholesky.641 = f32[128,128]{1,0:T(8,128)S(1)} custom-call(f32[128,128]{1,0:T(8,128)S(1)} %cholesky.711), custom_call_target="Cholesky" | custom-call | tf_op jit(solution)/shard_map/jit(cholesky)/cholesky | solution.py:75
  624.5 12.1 %cholesky.658 = f32[128,128]{1,0:T(8,128)S(1)} custom-call(f32[128,128]{1,0:T(8,128)S(1)} %convolution_subtract_fusion.16), custom_call_target="Cholesky" | custom-call | tf_op jit(solution)/shard_map/jit(cholesky)/cholesky | solution.py:75
  643.4 17.6 %while.9 = (s32[]{:T(128)}, f32[768,768]{1,0:T(8,128)}, s32[6,2]{0,1:T(2,128)S(1)}, f32[6,128,128]{2,1,0:T(8,128)S(1)}, s32[]{:T(128)}) while((s32[]{:T(128)}, f32[768,768]{1,0:T(8,128)}, s32[6,2]{0,1:T(2,128)S(1)}, f32[6,128,128]{2,1,0:T(8,128)S(1)}, s32[]{:T(128)}) %tuple.112), condition=%wide.while_cond.3.clone, body=%wide.while_body.3.clone.sunk | while | flops 2 | bytes 131189 | solution.py:77
  661.0 59.0 %custom-call.56 = f32[6,128,128]{1,2,0:T(8,128)S(1)} custom-call(f32[6,128,128]{2,1,0:T(8,128)S(1)} %get-tuple-element.64), custom_call_target="InvertDiagBlocksLowerTriangular" | custom-call | tf_op jit(solution)/shard_map/triangular_solve/custom-call.5 | solution.py:77
  786.7 13.4 %all-gather.7.cloned.1.call-done = f32[1536,1536]{0,1:T(8,128)} async-done(((f32[768,1536]{0,1:T(8,128)}), f32[1536,1536]{0,1:T(8,128)}) %all-gather.7.cloned.1.call-update) | async-done | bytes 9437200 | tf_op jit(solution)/shard_map/all_gather | solution.py:8
  802.4 12.6 %pad_add_fusion = f32[768,1536]{0,1:T(8,128)S(1)} fusion(f32[768,768]{0,1:T(8,128)S(1)} %fusion.55, f32[768,1536]{0,1:T(8,128)S(1)} %slice-done, s32[]{:T(128)S(6)} %select_n.68, pred[]{:T(512)S(6)} %le.7), kind=kOutput, calls=%fused_computation.13 | convolution fusion | flops 10873405440 | bytes 14155781 | tf_op jit(solution)/shard_map/dot_general | solution.py:97
  832.0 12.2 %gather_fusion.1 = f32[768]{0:T(1024)S(1)} fusion(f32[768,768]{1,0:T(8,128)} %get-tuple-element.97, s32[768]{0:T(1024)S(1)} %or_reduce_fusion), kind=kCustom, calls=%fused_computation.1 | custom fusion | bytes 12288 | tf_op jit(solution)/shard_map/jit(diagonal)/cond/branch_0_fun/gather | solution.py:80
  856.4 74.3 %collective-permute-done = f32[768,1536]{0,1:T(8,128)} collective-permute-done((f32[768,1536]{0,1:T(8,128)}, f32[768,1536]{0,1:T(8,128)}, u32[]{:S(2)}, u32[]{:S(2)}) %collective-permute-start) | collective-permute-done | bytes 4718624 | tf_op jit(solution)/shard_map/ppermute | solution.py:24
  (239 shorter events, 413.0 us)
Async XLA Ops:
  10.1 36.1 %all-to-all-start.1 = ((f32[64,2,16]{2,1,0:T(2,128)}), f32[64,2,16]{2,1,0:T(2,128)S(1)}, u32[]{:S(2)}, u32[]{:S(2)}) async-start(f32[64,2,16]{2,1,0:T(2,128)} %bitcast.6), calls=%async_computation.1 | async-start | bytes 131072 | tf_op jit(solution)/shard_map/all_to_all | solution.py:57
  46.2 91.4 %all-to-all-start = ((f32[64,2,16,768]{3,2,1,0:T(8,128)}), f32[64,2,16,768]{3,2,1,0:T(8,128)}, u32[]{:S(2)}, u32[]{:S(2)}) async-start(f32[64,2,16,768]{3,2,1,0:T(8,128)} %bitcast.193), calls=%async_computation | async-start | bytes 12582912 | tf_op jit(solution)/shard_map/all_to_all | solution.py:56
  56.8 419.4 %all-gather.5.cloned.1.call-start = ((), (), s32[]{:S(2)}) async-start(), calls=%async_computation.3 | async-start | bytes 14155776 | tf_op jit(solution)/shard_map/all_gather | solution.py:8
  57.0 6.1 copy-start.20
  57.1 6.9 copy-start.21
  137.6 20.7 %copy-start = (f32[768,1536]{0,1:T(8,128)S(1)}, f32[768,1536]{0,1:T(8,128)}, u32[]{:S(2)}) copy-start(f32[768,1536]{0,1:T(8,128)} %get-tuple-element.109) | copy-start | bytes 14155780
  137.6 20.7 %copy-start.2 = (f32[768,1536]{0,1:T(8,128)S(1)}, f32[768,1536]{0,1:T(8,128)}, u32[]{:S(2)}) copy-start(f32[768,1536]{0,1:T(8,128)} %get-tuple-element.108) | copy-start | bytes 14155780
  159.2 3.6 copy-start.1
  159.2 5.0 copy-start.3
  440.4 3.3 copy-start.10
  440.4 4.3 copy-start.12
  443.7 2.8 copy-start.14
  444.7 2.8 copy-start.18
  449.1 350.9 %all-gather.7.cloned.1.call-start = ((), (), s32[]{:S(2)}) async-start(), calls=%async_computation.4 | async-start | bytes 14155776 | tf_op jit(solution)/shard_map/all_gather | solution.py:8
  478.8 15.9 %copy-start.4 = (f32[768,1536]{0,1:T(8,128)}, f32[768,1536]{0,1:T(8,128)S(1)}, u32[]{:S(2)}) copy-start(f32[768,1536]{0,1:T(8,128)S(1)} %slice.317) | copy-start | bytes 14155780
  495.1 2.2 copy-start.5
  765.1 3.5 copy-start.11
  765.1 4.5 copy-start.13
  768.6 2.8 copy-start.15
  769.6 2.8 copy-start.19
  800.1 2.3 slice-start
  815.0 5.3 copy-start.6
  815.0 9.3 copy-start.7
  820.3 110.4 %collective-permute-start = (f32[768,1536]{0,1:T(8,128)}, f32[768,1536]{0,1:T(8,128)}, u32[]{:S(2)}, u32[]{:S(2)}) collective-permute-start(f32[768,1536]{0,1:T(8,128)} %get-tuple-element.105), channel_id=1, source_target_pairs={{2,0},{4,2},{6,4},{8,6},{10,8},{12,10},{14,12},{16,14},{18,16},{20... | collective-permute-start | bytes 14155784 | tf_op jit(solution)/shard_map/ppermute | solution.py:24
  (5 other events, 5.3 us)
Sparse Core Ops, SparseCore 0:
  449.3 26.8 all-gather.4
  774.2 25.8 all-gather.6
where the time goes:
time: 959 us; the launch traced here: 953 us
  other arithmetic  406 us (42%)
  waiting for transfers between devices  180 us (19%)
  matrix products  162 us (17%)
  local copies, waits for them, and re-layouts  148 us (15%)
  between operations  29.7 us (3%)
  starting transfers between devices  24.7 us (3%)
    another operation x45, other arithmetic, on_device(): lower_factor = jnp.linalg.cholesky(diag_tile)  248 us
    another operation x5, other arithmetic, on_device(): lax.linalg.triangular_solve(lower_factor, seeded, left_side=True, lower=T...  123 us
    another operation x22, matrix products, on_device(): lax.linalg.triangular_solve(lower_factor, seeded, left_side=True, lower=T...  83.9 us
    ppermute x1, waiting for transfers between devices, from_behind(): return lax.ppermute(block, axis, route)  74.3 us
    all_to_all x1, waiting for transfers between devices, on_device(): lax.all_to_all(send_values, 'tm', split_axis=0, concat_axis=0, tiled=True)  65.1 us
    another operation x49, local copies, waits for them, and re-layouts, on_device(): lax.linalg.triangular_solve(lower_factor, seeded, left_side=True, lower=T...  47.7 us
    unnamed x61, local copies, waits for them, and re-layouts  43 us
    all_gather x2, waiting for transfers between devices, from_root(): lax.all_gather(shard, axis)  40.4 us
  transfers between devices with their start and end apart: 5, of which 4 were waited for; matrix products, arithmetic and copies ran while one was open for 8% of the time, Pallas kernels for 0%

commit v1 on v0

v1 whole, which is shorter than its diff:
```python
import functools

import jax
import jax.numpy as jnp
from jax import lax
from jax.experimental import pallas as pl
from jax.experimental.pallas import tpu as pltpu
from jax.sharding import PartitionSpec as P

F32, BF16 = jnp.float32, jnp.bfloat16
BASE = 128
MIB = 1 << 20
NN = (((1,), (0,)), ((), ()))
NT = (((1,), (1,)), ((), ()))
TN = (((0,), (0,)), ((), ()))


def halves(x):
    high = x.astype(BF16)
    return high, (x - high.astype(F32)).astype(BF16)


def product(a, b, dims):
    dot = functools.partial(lax.dot_general, dimension_numbers=dims, preferred_element_type=F32)
    return dot(a[0], b[0]) + (dot(a[0], b[1]) + dot(a[1], b[0]))


def reorder_kernel(steps, weights_t, values, interior, separator, held, in_sems, out_sems):
    tiles = held.shape[0]
    chunks = in_sems.shape[0]
    per = tiles // chunks
    for chunk in range(chunks):
        rows = pl.ds(chunk * per, per)
        pltpu.make_async_copy(values.at[rows], held.at[rows], in_sems.at[chunk]).start()
    root = jnp.sqrt(weights_t[...])
    for chunk in range(chunks):
        rows = pl.ds(chunk * per, per)
        pltpu.make_async_copy(values.at[rows], held.at[rows], in_sems.at[chunk]).wait()
        for tile in range(chunk * per, (chunk + 1) * per):
            held[tile] = held[tile] * root[:, tile : tile + 1]
            step = steps[tile]
            partition = lax.shift_right_logical(step, 1)
            odd = lax.bitwise_and(step, 1)

            @pl.when(odd == 0)
            def _():
                pltpu.make_async_copy(held.at[tile], interior.at[partition], out_sems.at[0]).start()

            @pl.when(odd == 1)
            def _():
                pltpu.make_async_copy(held.at[tile], separator.at[partition], out_sems.at[1]).start()

    half = pl.ds(0, tiles // 2)
    pltpu.make_async_copy(held.at[half], interior, out_sems.at[0]).wait()
    pltpu.make_async_copy(held.at[half], separator, out_sems.at[1]).wait()


def reorder(steps, weights_t, values):
    tiles, rows, cols = values.shape
    half = jax.ShapeDtypeStruct((tiles // 2, rows, cols), F32)
    anywhere = pl.BlockSpec(memory_space=pl.ANY)
    return pl.pallas_call(
        reorder_kernel,
        out_shape=(half, half),
        in_specs=[
            pl.BlockSpec(memory_space=pltpu.SMEM),
            pl.BlockSpec(memory_space=pltpu.VMEM),
            anywhere,
        ],
        out_specs=(anywhere, anywhere),
        scratch_shapes=[
            pltpu.VMEM((tiles, rows, cols), F32),
            pltpu.SemaphoreType.DMA((8,)),
            pltpu.SemaphoreType.DMA((2,)),
        ],
        compiler_params=pltpu.CompilerParams(vmem_limit_bytes=16 * MIB),
        name="reorder",
    )(steps, weights_t, values)


def wide(x):
    return jnp.broadcast_to(x, (8, BASE))


def sweep_small(entries, size):
    at = lambda i, j: (min(i, j), max(i, j))
    dets = []
    for p in range(0, size, 2):
        a, b, d = entries[p, p], entries[p, p + 1], entries[p + 1, p + 1]
        det = a * d - b * b
        dets.append(det)
        scale = 1.0 / det
        inv_a, inv_b, inv_d = d * scale, b * scale, a * scale
        others = [i for i in range(size) if i not in (p, p + 1)]
        u = {i: entries[at(i, p)] for i in others}
        v = {i: entries[at(i, p + 1)] for i in others}
        new_u = {i: inv_a * u[i] - inv_b * v[i] for i in others}
        new_v = {i: inv_d * v[i] - inv_b * u[i] for i in others}
        for i in others:
            for j in others:
                if i <= j:
                    entries[i, j] = entries[i, j] - u[i] * new_u[j] - v[i] * new_v[j]
        for i in others:
            entries[at(i, p)] = new_u[i]
            entries[at(i, p + 1)] = new_v[i]
        entries[p, p], entries[p, p + 1], entries[p + 1, p + 1] = -inv_a, inv_b, -inv_d
    return dets


def sweep_base(x):
    lane = lax.broadcasted_iota(jnp.int32, (8, BASE), 1)
    sub = lax.broadcasted_iota(jnp.int32, (8, BASE), 0)
    x = list(x)
    groups = len(x)
    dets = jnp.ones((8, BASE), F32)
    for q in range(groups):
        panel = x[q]
        inside = (lane // 8) == q
        first = 8 * q
        entries = {
            (i, j): wide(panel[i : i + 1, first + j : first + j + 1])
            for i in range(8)
            for j in range(i, 8)
        }
        marked = jnp.where(inside, jnp.where(lane == first + sub, -1.0, 0.0), panel)
        rows = [wide(marked[j : j + 1, :]) for j in range(8)]
        for at, det in enumerate(sweep_small(entries, 8)):
            dets = jnp.where(lane == 4 * q + at, det, dets)
        new_rows = []
        for i in range(8):
            total = entries[0, i] * rows[0]
            for j in range(1, 8):
                total = total + entries[min(i, j), max(i, j)] * rows[j]
            new_rows.append(total)
        new_panel = new_rows[7]
        for i in range(7):
            new_panel = jnp.where(sub == i, new_rows[i], new_panel)
        for i in [(q + d) % groups for d in range(1, groups)]:
            total = jnp.where(inside, 0.0, x[i])
            for j in range(8):
                total = total + wide(x[i][:, first + j : first + j + 1]) * new_rows[j]
            x[i] = total
        x[q] = -new_panel
    return x, dets


def unit_scales(m, size):
    eye = lax.broadcasted_iota(jnp.int32, (BASE, BASE), 0) == lax.broadcasted_iota(
        jnp.int32, (BASE, BASE), 1
    )
    columns, rows = [], []
    for k in range(size // BASE):
        here = pl.ds(k * BASE, BASE)
        diagonal = jnp.where(eye, m[here, here], 0.0)
        columns.append(lax.rsqrt(jnp.sum(diagonal, axis=1, keepdims=True)))
        rows.append(lax.rsqrt(jnp.sum(diagonal, axis=0, keepdims=True)))
    return columns, jnp.concatenate(rows, axis=1)


def invert(m, panel, left, right, size):
    def step(k, logs):
        here = pl.ds(pl.multiple_of(k * BASE, BASE), BASE)
        groups = [
            m[pl.ds(pl.multiple_of(k * BASE + 8 * q, 8), 8), here] for q in range(BASE // 8)
        ]
        swept, dets = sweep_base(groups)
        swept = jnp.concatenate(swept, axis=0)
        inverse = halves(-swept)
        panel[...] = product(inverse, halves(m[here, :]), NN)
        panel[:, here] = swept
        high, low = halves(panel[...])
        right[0, :BASE], right[0, BASE:] = high, high
        right[1, :BASE], right[1, BASE:] = low, low
        high, low = halves(m[:, here])
        left[:, :BASE], left[:, BASE:] = high, low
        m[:, here] = jnp.zeros((size, BASE), F32)
        rows = 256
        for first in range(0, size, rows):
            part = left[first : first + rows, :]
            dot = functools.partial(lax.dot_general, dimension_numbers=NN, preferred_element_type=F32)
            m[first : first + rows, :] -= dot(part, right[0]) + dot(part, right[1])
        m[here, :] = panel[...]
        return logs + jnp.log(dets[0:1, :])

    logs = lax.fori_loop(0, size // BASE, step, jnp.zeros((1, BASE), F32))
    return jnp.sum(logs, axis=1, keepdims=True)


def own_kernel(place, time_diag, tiles, prior, block, inverse, logdet, split, panel, left, right):
    size = block.shape[0]
    own = place[0]
    scale = time_diag[0]
    high, low = halves(tiles[...])
    split[0], split[1] = high, low
    rows = 256
    for first in range(0, size, rows):
        part = (split[0, :, first : first + rows], split[1, :, first : first + rows])
        gram = product(part, (split[0], split[1]), TN)
        columns = pl.ds(pl.multiple_of(own * size, size), size)
        block[first : first + rows, :] = scale * prior[first : first + rows, columns] + gram
    by_row, by_column = unit_scales(block, size)
    for k, row_scale in enumerate(by_row):
        here = pl.ds(k * BASE, BASE)
        inverse[here, :] = block[here, :] * row_scale * by_column
    log_total = invert(inverse, panel, left, right, size)
    logdet[...] = log_total - 2.0 * jnp.sum(jnp.log(by_column), axis=1, keepdims=True)
    for k, row_scale in enumerate(by_row):
        here = pl.ds(k * BASE, BASE)
        inverse[here, :] = inverse[here, :] * (-row_scale) * by_column


def scratch_of(size):
    return [
        pltpu.VMEM((BASE, size), F32),
        pltpu.VMEM((size, 2 * BASE), BF16),
        pltpu.VMEM((2, 2 * BASE, size), BF16),
    ]


def invert_own(place, time_diag, tiles, prior):
    size = prior.shape[0]
    square = jax.ShapeDtypeStruct((size, size), F32)
    smem = pl.BlockSpec(memory_space=pltpu.SMEM)
    vmem = pl.BlockSpec(memory_space=pltpu.VMEM)
    return pl.pallas_call(
        own_kernel,
        out_shape=(square, square, jax.ShapeDtypeStruct((1, 1), F32)),
        in_specs=[smem, smem, vmem, vmem],
        out_specs=(vmem, vmem, vmem),
        scratch_shapes=[pltpu.VMEM((2, *tiles.shape), BF16)] + scratch_of(size),
        compiler_params=pltpu.CompilerParams(vmem_limit_bytes=48 * MIB),
        cost_estimate=pl.CostEstimate(flops=40 * size**3, bytes_accessed=16 * MIB, transcendentals=0),
        name="invert_own",
    )(place, time_diag, tiles, prior)


def rest_kernel(
    place, time_diag, other_inverse, block, prior, gain_row, gain_column, schur, logdet,
    reached, work, split_a, split_b, panel, left, right,
):
    size = block.shape[0]
    own = place[0]
    scale = time_diag[0]
    own_columns = pl.ds(pl.multiple_of(own * size, size), size)
    other_columns = pl.ds(pl.multiple_of((1 - own) * size, size), size)
    split_a[0], split_a[1] = halves(scale * prior[:, other_columns])
    split_b[0], split_b[1] = halves(other_inverse[...])
    rows = 256
    for first in range(0, size, rows):
        here = slice(first, first + rows)
        reached[here, :] = product((split_a[0, here], split_a[1, here]), (split_b[0], split_b[1]), NN)
        part = halves(reached[here, :])
        work[here, :] = block[here, :] - product(part, (split_a[0], split_a[1]), NT)
    by_row, by_column = unit_scales(work, size)
    for k, row_scale in enumerate(by_row):
        here = pl.ds(k * BASE, BASE)
        work[here, :] = work[here, :] * row_scale * by_column
    log_total = invert(work, panel, left, right, size)
    logdet[...] = log_total - 2.0 * jnp.sum(jnp.log(by_column), axis=1, keepdims=True)
    split_b[0], split_b[1] = halves(reached[...])
    own_gain = gain_row[:, own_columns]
    other_gain = gain_row[:, other_columns]
    for k, row_scale in enumerate(by_row):
        here = pl.ds(k * BASE, BASE)
        rows_out = work[here, :] * (-row_scale * gain_column[here, :]) * by_column
        schur[here, own_columns] = rows_out * own_gain
        schur[here, other_columns] = product(halves(rows_out), (split_b[0], split_b[1]), NN) * -other_gain


def invert_rest(place, time_diag, other_inverse, block, prior, gain_row, gain_column):
    size = prior.shape[0]
    smem = pl.BlockSpec(memory_space=pltpu.SMEM)
    vmem = pl.BlockSpec(memory_space=pltpu.VMEM)
    return pl.pallas_call(
        rest_kernel,
        out_shape=(jax.ShapeDtypeStruct(prior.shape, F32), jax.ShapeDtypeStruct((1, 1), F32)),
        in_specs=[smem, smem] + [vmem] * 5,
        out_specs=(vmem, vmem),
        scratch_shapes=[
            pltpu.VMEM((size, size), F32),
            pltpu.VMEM((size, size), F32),
            pltpu.VMEM((2, size, size), BF16),
            pltpu.VMEM((2, size, size), BF16),
        ]
        + scratch_of(size),
        compiler_params=pltpu.CompilerParams(vmem_limit_bytes=48 * MIB),
        cost_estimate=pl.CostEstimate(flops=40 * size**3, bytes_accessed=16 * MIB, transcendentals=0),
        name="invert_rest",
    )(place, time_diag, other_inverse, block, prior, gain_row, gain_column)


def separator_kernel(place, time_diag, rho, tiles, prior, schur, reduced, coupling, split):
    size = prior.shape[0]
    own = place[0]
    split[0], split[1] = halves(tiles[...])
    own_columns = pl.ds(pl.multiple_of(own * size, size), size)
    other_columns = pl.ds(pl.multiple_of((1 - own) * size, size), size)
    rows = 256
    for first in range(0, size, rows):
        here = slice(first, first + rows)
        gram = product((split[0, :, here], split[1, :, here]), (split[0], split[1]), TN)
        for columns, term in ((own_columns, gram), (other_columns, 0.0)):
            part = schur[here, columns]
            reduced[here, columns] = time_diag[1] * prior[here, columns] + term - rho[1] * rho[1] * part
            coupling[here, columns] = -(rho[0] * rho[1]) * part


def separator_rows(place, time_diag, rho, tiles, prior, schur):
    out = jax.ShapeDtypeStruct(prior.shape, F32)
    smem = pl.BlockSpec(memory_space=pltpu.SMEM)
    vmem = pl.BlockSpec(memory_space=pltpu.VMEM)
    return pl.pallas_call(
        separator_kernel,
        out_shape=(out, out),
        in_specs=[smem] * 3 + [vmem] * 3,
        out_specs=(vmem, vmem),
        scratch_shapes=[pltpu.VMEM((2, *tiles.shape), BF16)],
        compiler_params=pltpu.CompilerParams(vmem_limit_bytes=48 * MIB),
        cost_estimate=pl.CostEstimate(flops=6 * prior.size * tiles.shape[0], bytes_accessed=24 * MIB, transcendentals=0),
        name="separator",
    )(place, time_diag, rho, tiles, prior, schur)


def from_next(x):
    count = lax.axis_size("tm")
    return lax.ppermute(x, "tm", [(i, i - 1) for i in range(1, count)])


def from_other(x):
    return lax.ppermute(x, "tile", [(0, 1), (1, 0)])


def to_partitions(x):
    return lax.all_to_all(x, "tm", split_axis=0, concat_axis=0, tiled=True).reshape(-1, x.shape[-1])


def on_device(prior, node_gain, time_diag, rho, values, weights, steps):
    size, nodes = prior.shape
    own = lax.axis_index("tile")
    place = own.reshape(1).astype(jnp.int32)
    interior, separator = reorder(steps[0, 0], weights[0].T, values[0])
    next_rho = from_next(rho)
    gain_row = node_gain.reshape(1, nodes)
    gain_column = lax.dynamic_slice_in_dim(node_gain, own * size, size).reshape(size, 1)
    interior = to_partitions(interior)
    interior, separator = lax.optimization_barrier((interior, separator))
    separator = to_partitions(separator)
    block, own_inverse, own_log = invert_own(place, time_diag, interior, prior)
    other_inverse = from_other(own_inverse)
    schur, rest_log = invert_rest(place, time_diag, other_inverse, block, prior, gain_row, gain_column)
    incoming = from_next(schur)
    log = jnp.where(own == 0, own_log, rest_log).reshape(1)
    interior_logdet = (log + from_other(log)) / nodes
    reduced, coupling = separator_rows(place, time_diag, rho, separator, prior, schur)
    separator_block = reduced - next_rho[0] * next_rho[0] * incoming
    return separator_block[None], coupling[None], interior_logdet


def solution(mesh):
    in_specs = (
        P("tile", None),
        P(),
        P("tm"),
        P("tm"),
        P("tile", "tm", None, None),
        P("tile", "tm", None),
        P("tile", "tm", None),
    )
    out_specs = (P("tm", "tile", None), P("tm", "tile", None), P("tm"))
    return jax.shard_map(on_device, mesh=mesh, in_specs=in_specs, out_specs=out_specs, check_vma=False)
```

time: 959 us -> 345 us (0.36)
  other arithmetic: 406 us -> 7 us
  matrix products: 162 us -> 0 us
  local copies, waits for them, and re-layouts: 148 us -> 9.12 us
  Pallas kernels: 0 us -> 115 us
  between operations: 29.7 us -> 3.65 us
    another operation x51 -> x0, other arithmetic: 372 us -> none  [the longest x45 248 us: on_device(): lower_factor = jnp.linalg.cholesky(diag_tile)]
    pallas_call x0 -> x4, Pallas kernels: none -> 115 us  [the longest x1 53.4 us: invert_rest(): pl.pallas_call(rest_kernel, out_shape=(jax.ShapeDtypeStruct(prior.shape,...]
    another operation x42 -> x0, matrix products: 104 us -> none  [the longest x22 83.9 us: on_device(): lax.linalg.triangular_solve(lower_factor, seeded, left_side=True, lower=T...]
    ppermute x1 -> x4, waiting for transfers between devices: 74.3 us -> 144 us  [the longest x2 139 us: from_next(): return lax.ppermute(x, 'tm', [(i, i - 1) for i in range(1, count)])]
    dot_general x4 -> x0, matrix products: 58.1 us -> none  [the longest x2 21.5 us: on_device(): jnp.dot(local_columns.T, rows_of_panel[:, :boundary_column], precision=pr...]
    another operation x61 -> x0, local copies, waits for them, and re-layouts: 48.1 us -> none  [the longest x49 47.7 us: on_device(): lax.linalg.triangular_solve(lower_factor, seeded, left_side=True, lower=T...]
    all_gather x2 -> x0, waiting for transfers between devices: 40.4 us -> none  [from_root(): lax.all_gather(shard, axis)]
    unnamed x61 -> x18, local copies, waits for them, and re-layouts: 43 us -> 8.88 us
  transfers between devices with their start and end apart: 5 -> 6, of which waited for: 4 -> 4; matrix products, arithmetic and copies ran while one was open for 8% -> 0% of each run, Pallas kernels for 0% -> 4%
where the time goes in v1:
time: 345 us; the launch traced here: 344 us
  waiting for transfers between devices  182 us (53%)
  Pallas kernels  115 us (33%)
  starting transfers between devices  28.3 us (8%)
  local copies, waits for them, and re-layouts  9.12 us (3%)
  other arithmetic  7 us (2%)
  between operations  3.65 us (1%)
    ppermute x2, waiting for transfers between devices, from_next(): return lax.ppermute(x, 'tm', [(i, i - 1) for i in range(1, count)])  139 us
    pallas_call x1, Pallas kernels, invert_rest(): pl.pallas_call(rest_kernel, out_shape=(jax.ShapeDtypeStruct(prior.shape,...  53.4 us
    pallas_call x1, Pallas kernels, invert_own(): pl.pallas_call(own_kernel, out_shape=(square, square, jax.ShapeDtypeStruc...  45.3 us
    all_to_all x2, waiting for transfers between devices, to_partitions(): lax.all_to_all(x, 'tm', split_axis=0, concat_axis=0, tiled=True)  37.9 us
    all_to_all x2, starting transfers between devices, to_partitions(): lax.all_to_all(x, 'tm', split_axis=0, concat_axis=0, tiled=True)  21.1 us
    pallas_call x1, Pallas kernels, separator_rows(): pl.pallas_call(separator_kernel, out_shape=(out, out), in_specs=[smem] *...  12.1 us
    unnamed x18, local copies, waits for them, and re-layouts  8.88 us
    broadcast_in_dim x1, other arithmetic, on_device(): return (separator_block[None], coupling[None], interior_logdet)  7 us
  transfers between devices with their start and end apart: 6, of which 4 were waited for; matrix products, arithmetic and copies ran while one was open for 0% of the time, Pallas kernels for 4%

profile of v1, /device:TPU:30, one launch (start us, length us, event | category | flops | bytes accessed | tf_op | source)
XLA Modules:
  0.0 344.4 jit_solution(12442629836939416529)
XLA Ops:
  0.6 2.8 copy-done
  3.4 0.7 copy-done.1
  4.1 0.7 copy-done.2
  4.8 3.7 %reorder.1 = (f32[64,16,768]{2,1,0:T(8,128)}, f32[64,16,768]{2,1,0:T(8,128)}) custom-call(s32[128]{0:T(128)S(1)} %bitcast.18, f32[16,128]{1,0:T(8,128)S(1)} %bitcast.17, f32[128,16,768]{2,1,0:T(8,128)S(1)} %bitcast.15), custom_call_target="tpu_custom_call" | custom-call | tf_op jit(solution)/shard_map/reorder/pallas_call | solution.py:62
  8.5 0.0 copy-start.3
  8.5 11.1 %all-to-all-start = ((f32[64,16,768]{2,1,0:T(8,128)}), f32[64,16,768]{2,1,0:T(8,128)S(1)}, u32[]{:S(2)}, u32[]{:S(2)}) async-start(f32[64,16,768]{2,1,0:T(8,128)} %get-tuple-element.14), calls=%async_computation | async-start | bytes 6291456 | tf_op jit(solution)/shard_map/all_to_all | solution.py:334
  19.6 37.9 %all-to-all-done = f32[64,16,768]{2,1,0:T(8,128)S(1)} async-done(((f32[64,16,768]{2,1,0:T(8,128)}), f32[64,16,768]{2,1,0:T(8,128)S(1)}, u32[]{:S(2)}, u32[]{:S(2)}) %all-to-all-start) | async-done | bytes 3145760 | tf_op jit(solution)/shard_map/all_to_all | solution.py:334
  57.5 1.7 copy-done.7
  59.2 45.3 %invert_own.1 = (f32[768,768]{1,0:T(8,128)S(1)}, f32[768,768]{1,0:T(8,128)S(1)}, f32[1,1]{1,0:T(1,128)}) custom-call(s32[1]{0:T(128)} %bitcast.place, f32[2]{0:T(128)S(1)} %copy-done.3, f32[1024,768]{1,0:T(8,128)} %bitcast.19, f32[768,1536]{1,0:T(8,128)} %prior.5), custom_call_target="tpu_custom_call" | custom-call | flops 18119393280 | bytes 16777216 | tf_op jit(solution)/shard_map/invert_own/pallas_call | solution.py:225
  104.6 1.4 copy-done.5
  106.0 0.0 collective-permute-start
  106.0 0.1 dynamic_slice.3
  106.1 0.2 reshape.32.gain_column
  106.2 4.4 %collective-permute-done.other_inverse = f32[768,768]{1,0:T(8,128)} collective-permute-done((f32[768,768]{1,0:T(8,128)S(1)}, f32[768,768]{1,0:T(8,128)}, u32[]{:S(2)}, u32[]{:S(2)}) %collective-permute-start) | collective-permute-done | bytes 2359328 | tf_op jit(solution)/shard_map/ppermute | solution.py:330
  110.6 1.7 copy-done.6
  112.3 53.4 %invert_rest.1 = (f32[768,1536]{1,0:T(8,128)}, f32[1,1]{1,0:T(1,128)}) custom-call(s32[1]{0:T(128)} %bitcast.place, f32[2]{0:T(128)S(1)} %copy-done.3, f32[768,768]{1,0:T(8,128)} %collective-permute-done.other_inverse, f32[768,768]{1,0:T(8,128)S(1)} %copy-done.6, f32[768,1536]{1,0:T(8,128)} %prior.5, f32[1,1536]{1,0:T(1,128)S(1)} %reshape.29.gain_row, ...), custom_call_target="tpu_custom_call" | custom-call | flops 18119393280 | bytes 16777216 | tf_op jit(solution)/shard_map/invert_rest/pallas_call | solution.py:274
  165.7 3.2 collective-permute-start.2
  168.9 10.0 %all-to-all-start.1 = ((f32[64,16,768]{2,1,0:T(8,128)}), f32[64,16,768]{2,1,0:T(8,128)S(1)}, u32[]{:S(2)}, u32[]{:S(2)}) async-start(f32[64,16,768]{2,1,0:T(8,128)} %get-tuple-element.16), calls=%async_computation.1 | async-start | bytes 6291456 | tf_op jit(solution)/shard_map/all_to_all | solution.py:334
  178.9 2.8 collective-permute-start.1
  181.7 139.1 %collective-permute-done.1 = f32[2]{0:T(128)S(1)} collective-permute-done((f32[2]{0:T(128)S(1)}, f32[2]{0:T(128)S(1)}, u32[]{:S(2)}, u32[]{:S(2)}) %collective-permute-start.1) | collective-permute-done | bytes 40 | tf_op jit(solution)/shard_map/ppermute | solution.py:326
  322.1 1.3 collective-permute-start.3
  323.3 0.3 collective-permute-done.3
  324.2 12.1 %separator.1 = (f32[768,1536]{1,0:T(8,128)}, f32[768,1536]{1,0:T(8,128)}) custom-call(s32[1]{0:T(128)} %bitcast.place, f32[2]{0:T(128)S(1)} %copy-done.3, f32[2]{0:T(128)S(1)} %copy-done.4, f32[1024,768]{1,0:T(8,128)S(1)} %bitcast.16, f32[768,1536]{1,0:T(8,128)} %prior.5, f32[768,1536]{1,0:T(8,128)} %get-tuple-element.20.schur), custom_call_target="tpu_custom_call" | custom-call | flops 7247757312 | bytes 25165824 | tf_op jit(solution)/shard_map/separator/pallas_call | solution.py:312
  336.3 7.0 %subtract_bitcast_fusion = f32[1,768,1536]{2,1,0:T(8,128)} fusion(f32[768,1536]{1,0:T(8,128)} %get-tuple-element.21, f32[768,1536]{1,0:T(8,128)} %collective-permute-done.2, f32[]{:T(128)} %bitcast.7), kind=kLoop, calls=%fused_computation | loop fusion | flops 2359296 | bytes 14155780 | tf_op jit(solution)/shard_map/broadcast_in_dim | solution.py:356
  (14 shorter events, 0.0 us)
Async XLA Ops:
  0.6 2.8 copy-start
  3.4 0.7 copy-start.1
  4.1 0.7 copy-start.2
  8.5 50.7 %copy-start.3 = (f32[2]{0:T(128)S(1)}, f32[2]{0:T(128)}, u32[]{:S(2)}) copy-start(f32[2]{0:T(128)} %time_diag.5) | copy-start | bytes 28
  8.5 49.0 %all-to-all-start = ((f32[64,16,768]{2,1,0:T(8,128)}), f32[64,16,768]{2,1,0:T(8,128)S(1)}, u32[]{:S(2)}, u32[]{:S(2)}) async-start(f32[64,16,768]{2,1,0:T(8,128)} %get-tuple-element.14), calls=%async_computation | async-start | bytes 6291456 | tf_op jit(solution)/shard_map/all_to_all | solution.py:334
  57.5 1.7 copy-start.7
  59.2 46.8 %copy-start.8 = (f32[1536]{0:T(1024)S(1)}, f32[1536]{0:T(1024)}, u32[]{:S(2)}) copy-start(f32[1536]{0:T(1024)} %param.8) | copy-start | bytes 18436
  104.6 1.4 copy-start.5
  106.0 4.7 %collective-permute-start = (f32[768,768]{1,0:T(8,128)S(1)}, f32[768,768]{1,0:T(8,128)}, u32[]{:S(2)}, u32[]{:S(2)}) collective-permute-start(f32[768,768]{1,0:T(8,128)S(1)} %get-tuple-element.18), channel_id=1, source_target_pairs={{0,1},{1,0},{2,3},{3,2},{4,5},{5,4},{6,7},{7,6},{8,9},{9,8},{10,11... | collective-permute-start | bytes 7077896 | tf_op jit(solution)/shard_map/ppermute | solution.py:330
  110.6 1.7 copy-start.6
  165.7 13.2 %copy-start.4 = (f32[2]{0:T(128)S(1)}, f32[2]{0:T(128)}, u32[]{:S(2)}) copy-start(f32[2]{0:T(128)} %rho.1) | copy-start | bytes 28
  165.7 170.6 %collective-permute-start.2 = (f32[768,1536]{1,0:T(8,128)}, f32[768,1536]{1,0:T(8,128)}, u32[]{:S(2)}, u32[]{:S(2)}) collective-permute-start(f32[768,1536]{1,0:T(8,128)} %get-tuple-element.20.schur), channel_id=1, source_target_pairs={{2,0},{4,2},{6,4},{8,6},{10,8},{12,10},{14,12},{16,14},{18,16},{20... | collective-permute-start | bytes 14155784 | tf_op jit(solution)/shard_map/ppermute | solution.py:326
  168.9 155.3 %all-to-all-start.1 = ((f32[64,16,768]{2,1,0:T(8,128)}), f32[64,16,768]{2,1,0:T(8,128)S(1)}, u32[]{:S(2)}, u32[]{:S(2)}) async-start(f32[64,16,768]{2,1,0:T(8,128)} %get-tuple-element.16), calls=%async_computation.1 | async-start | bytes 6291456 | tf_op jit(solution)/shard_map/all_to_all | solution.py:334
  178.9 141.9 %collective-permute-start.1 = (f32[2]{0:T(128)S(1)}, f32[2]{0:T(128)S(1)}, u32[]{:S(2)}, u32[]{:S(2)}) collective-permute-start(f32[2]{0:T(128)S(1)} %copy-done.4), channel_id=1, source_target_pairs={{2,0},{4,2},{6,4},{8,6},{10,8},{12,10},{14,12},{16,14},{18,16},{20... | collective-permute-start | bytes 32 | tf_op jit(solution)/shard_map/ppermute | solution.py:326
  322.1 1.6 collective-permute-start.3

commit v2 on v1

--- a/solution.py
+++ b/solution.py
@@ -73,7 +73,7 @@
             pltpu.SemaphoreType.DMA((8,)),
             pltpu.SemaphoreType.DMA((2,)),
         ],
-        compiler_params=pltpu.CompilerParams(vmem_limit_bytes=16 * MIB),
+        compiler_params=pltpu.CompilerParams(vmem_limit_bytes=56 * MIB),
         name="reorder",
     )(steps, weights_t, values)
 
@@ -157,7 +157,7 @@
     return columns, jnp.concatenate(rows, axis=1)
 
 
-def invert(m, panel, left, right, size):
+def invert(m, panel, left, right, size, pivots):
     def step(k, logs):
         here = pl.ds(pl.multiple_of(k * BASE, BASE), BASE)
         groups = [
@@ -174,7 +174,7 @@
         high, low = halves(m[:, here])
         left[:, :BASE], left[:, BASE:] = high, low
         m[:, here] = jnp.zeros((size, BASE), F32)
-        rows = 256
+        rows = 256 if size % 256 == 0 else BASE
         for first in range(0, size, rows):
             part = left[first : first + rows, :]
             dot = functools.partial(lax.dot_general, dimension_numbers=NN, preferred_element_type=F32)
@@ -182,7 +182,7 @@
         m[here, :] = panel[...]
         return logs + jnp.log(dets[0:1, :])
 
-    logs = lax.fori_loop(0, size // BASE, step, jnp.zeros((1, BASE), F32))
+    logs = lax.fori_loop(0, pivots // BASE, step, jnp.zeros((1, BASE), F32))
     return jnp.sum(logs, axis=1, keepdims=True)
 
 
@@ -202,7 +202,7 @@
     for k, row_scale in enumerate(by_row):
         here = pl.ds(k * BASE, BASE)
         inverse[here, :] = block[here, :] * row_scale * by_column
-    log_total = invert(inverse, panel, left, right, size)
+    log_total = invert(inverse, panel, left, right, size, size)
     logdet[...] = log_total - 2.0 * jnp.sum(jnp.log(by_column), axis=1, keepdims=True)
     for k, row_scale in enumerate(by_row):
         here = pl.ds(k * BASE, BASE)
@@ -234,15 +234,11 @@
     )(place, time_diag, tiles, prior)
 
 
-def rest_kernel(
-    place, time_diag, other_inverse, block, prior, gain_row, gain_column, schur, logdet,
-    reached, work, split_a, split_b, panel, left, right,
-):
+def head_kernel(place, time_diag, other_inverse, block, prior, reached, early, rest, logdet, work, split_a, split_b, panel, left, right):
     size = block.shape[0]
-    own = place[0]
+    head = early.shape[1]
     scale = time_diag[0]
-    own_columns = pl.ds(pl.multiple_of(own * size, size), size)
-    other_columns = pl.ds(pl.multiple_of((1 - own) * size, size), size)
+    other_columns = pl.ds(pl.multiple_of((1 - place[0]) * size, size), size)
     split_a[0], split_a[1] = halves(scale * prior[:, other_columns])
     split_b[0], split_b[1] = halves(other_inverse[...])
     rows = 256
@@ -255,70 +251,255 @@
     for k, row_scale in enumerate(by_row):
         here = pl.ds(k * BASE, BASE)
         work[here, :] = work[here, :] * row_scale * by_column
-    log_total = invert(work, panel, left, right, size)
-    logdet[...] = log_total - 2.0 * jnp.sum(jnp.log(by_column), axis=1, keepdims=True)
-    split_b[0], split_b[1] = halves(reached[...])
-    own_gain = gain_row[:, own_columns]
-    other_gain = gain_row[:, other_columns]
+    log_total = invert(work, panel, left, right, size, head)
+    by_head = by_column[:, :head]
+    logdet[...] = log_total - 2.0 * jnp.sum(jnp.log(by_head), axis=1, keepdims=True)
+    back = 1.0 / by_column[:, head:]
     for k, row_scale in enumerate(by_row):
         here = pl.ds(k * BASE, BASE)
-        rows_out = work[here, :] * (-row_scale * gain_column[here, :]) * by_column
-        schur[here, own_columns] = rows_out * own_gain
-        schur[here, other_columns] = product(halves(rows_out), (split_b[0], split_b[1]), NN) * -other_gain
-
-
-def invert_rest(place, time_diag, other_inverse, block, prior, gain_row, gain_column):
+        if k * BASE < head:
+            early[here, :] = work[here, :head] * (-row_scale) * by_head
+        else:
+            row_back = 1.0 / row_scale
+            early[here, :] = work[here, :head] * row_back * by_head
+            rest[pl.ds(k * BASE - head, BASE), :] = work[here, head:] * row_back * back
+
+
+def invert_head(place, time_diag, other_inverse, block, prior, head):
     size = prior.shape[0]
+    shape = lambda *dims: jax.ShapeDtypeStruct(dims, F32)
     smem = pl.BlockSpec(memory_space=pltpu.SMEM)
     vmem = pl.BlockSpec(memory_space=pltpu.VMEM)
     return pl.pallas_call(
-        rest_kernel,
-        out_shape=(jax.ShapeDtypeStruct(prior.shape, F32), jax.ShapeDtypeStruct((1, 1), F32)),
-        in_specs=[smem, smem] + [vmem] * 5,
-        out_specs=(vmem, vmem),
+        head_kernel,
+        out_shape=(shape(size, size), shape(size, head), shape(size - head, size - head), shape(1, 1)),
+        in_specs=[smem, smem] + [vmem] * 3,
+        out_specs=(vmem,) * 4,
         scratch_shapes=[
-            pltpu.VMEM((size, size), F32),
             pltpu.VMEM((size, size), F32),
             pltpu.VMEM((2, size, size), BF16),
             pltpu.VMEM((2, size, size), BF16),
         ]
         + scratch_of(size),
-        compiler_params=pltpu.CompilerParams(vmem_limit_bytes=48 * MIB),
-        cost_estimate=pl.CostEstimate(flops=40 * size**3, bytes_accessed=16 * MIB, transcendentals=0),
-        name="invert_rest",
-    )(place, time_diag, other_inverse, block, prior, gain_row, gain_column)
-
-
-def separator_kernel(place, time_diag, rho, tiles, prior, schur, reduced, coupling, split):
+        compiler_params=pltpu.CompilerParams(vmem_limit_bytes=44 * MIB),
+        cost_estimate=pl.CostEstimate(flops=80 * size**3, bytes_accessed=16 * MIB, transcendentals=0),
+        name="invert_head",
+    )(place, time_diag, other_inverse, block, prior)
+
+
+def tail_kernel(rest, inverse, logdet, panel, left, right):
+    size = rest.shape[0]
+    by_row, by_column = unit_scales(rest, size)
+    for k, row_scale in enumerate(by_row):
+        here = pl.ds(k * BASE, BASE)
+        inverse[here, :] = rest[here, :] * row_scale * by_column
+    log_total = invert(inverse, panel, left, right, size, size)
+    logdet[...] = log_total - 2.0 * jnp.sum(jnp.log(by_column), axis=1, keepdims=True)
+    for k, row_scale in enumerate(by_row):
+        here = pl.ds(k * BASE, BASE)
+        inverse[here, :] = inverse[here, :] * (-row_scale) * by_column
+
+
+def invert_tail(rest):
+    size = rest.shape[0]
+    vmem = pl.BlockSpec(memory_space=pltpu.VMEM)
+    return pl.pallas_call(
+        tail_kernel,
+        out_shape=(jax.ShapeDtypeStruct(rest.shape, F32), jax.ShapeDtypeStruct((1, 1), F32)),
+        in_specs=[vmem],
+        out_specs=(vmem, vmem),
+        scratch_shapes=scratch_of(size),
+        compiler_params=pltpu.CompilerParams(vmem_limit_bytes=40 * MIB),
+        cost_estimate=pl.CostEstimate(flops=200 * size**3, bytes_accessed=4 * MIB, transcendentals=0),
+        name="invert_tail",
+    )(rest)
+
+
+def separator_kernel(place, time_diag, tiles, prior, assembled, split):
     size = prior.shape[0]
     own = place[0]
     split[0], split[1] = halves(tiles[...])
     own_columns = pl.ds(pl.multiple_of(own * size, size), size)
     other_columns = pl.ds(pl.multiple_of((1 - own) * size, size), size)
+    scale = time_diag[1]
     rows = 256
     for first in range(0, size, rows):
         here = slice(first, first + rows)
         gram = product((split[0, :, here], split[1, :, here]), (split[0], split[1]), TN)
-        for columns, term in ((own_columns, gram), (other_columns, 0.0)):
-            part = schur[here, columns]
-            reduced[here, columns] = time_diag[1] * prior[here, columns] + term - rho[1] * rho[1] * part
-            coupling[here, columns] = -(rho[0] * rho[1]) * part
-
-
-def separator_rows(place, time_diag, rho, tiles, prior, schur):
-    out = jax.ShapeDtypeStruct(prior.shape, F32)
+        assembled[here, own_columns] = scale * prior[here, own_columns] + gram
+        assembled[here, other_columns] = scale * prior[here, other_columns]
+
+
+def assemble_separator(place, time_diag, tiles, prior):
     smem = pl.BlockSpec(memory_space=pltpu.SMEM)
     vmem = pl.BlockSpec(memory_space=pltpu.VMEM)
     return pl.pallas_call(
         separator_kernel,
+        out_shape=jax.ShapeDtypeStruct(prior.shape, F32),
+        in_specs=[smem] * 2 + [vmem] * 2,
+        out_specs=vmem,
+        scratch_shapes=[pltpu.VMEM((2, *tiles.shape), BF16)],
+        compiler_params=pltpu.CompilerParams(vmem_limit_bytes=40 * MIB),
+        cost_estimate=pl.CostEstimate(
+            flops=6 * prior.size * tiles.shape[0], bytes_accessed=14 * MIB, transcendentals=0
+        ),
+        name="assemble_separator",
+    )(place, time_diag, tiles, prior)
+
+
+def rows_kernel(place, rho, tail, early, reached, assembled, gain_row, gain_column, reduced, coupling, mine, split_b):
+    size, head = early.shape
+    own = place[0]
+    tail_parts = halves(tail[...])
+    lower = early[head:, :]
+    split_b[0], split_b[1] = halves(reached[...])
+    mine[head:, :head] = -product(tail_parts, halves(lower), NN)
+    mine[head:, head:] = tail[...]
+    bottom = halves(mine[head:, :])
+    mine[:head, :] = -product(halves(lower), bottom, TN)
+    mine[:head, :head] += early[:head, :]
+    own_columns = pl.ds(pl.multiple_of(own * size, size), size)
+    other_columns = pl.ds(pl.multiple_of((1 - own) * size, size), size)
+    own_gain = gain_row[:, own_columns]
+    other_gain = gain_row[:, other_columns]
+    kept, sent = rho[1] * rho[1], rho[0] * rho[1]
+    rows = 256
+    for first in range(0, size, rows):
+        here = slice(first, first + rows)
+        part = mine[here, :] * gain_column[here, :]
+        here_own = part * own_gain
+        here_other = -product(halves(part), (split_b[0], split_b[1]), NN) * other_gain
+        for columns, schur in ((own_columns, here_own), (other_columns, here_other)):
+            reduced[here, columns] = assembled[here, columns] - kept * schur
+            coupling[here, columns] = -sent * schur
+
+
+def own_rows(place, rho, tail, early, reached, assembled, gain_row, gain_column):
+    size = early.shape[0]
+    out = jax.ShapeDtypeStruct(assembled.shape, F32)
+    smem = pl.BlockSpec(memory_space=pltpu.SMEM)
+    vmem = pl.BlockSpec(memory_space=pltpu.VMEM)
+    return pl.pallas_call(
+        rows_kernel,
         out_shape=(out, out),
-        in_specs=[smem] * 3 + [vmem] * 3,
+        in_specs=[smem] * 2 + [vmem] * 6,
         out_specs=(vmem, vmem),
-        scratch_shapes=[pltpu.VMEM((2, *tiles.shape), BF16)],
+        scratch_shapes=[pltpu.VMEM((size, size), F32), pltpu.VMEM((2, size, size), BF16)],
+        compiler_params=pltpu.CompilerParams(vmem_limit_bytes=44 * MIB),
+        cost_estimate=pl.CostEstimate(flops=20 * size**3, bytes_accessed=24 * MIB, transcendentals=0),
+        name="own_rows",
+    )(place, rho, tail, early, reached, assembled, gain_row, gain_column)
+
+
+def next_kernel(
+    place, scalars, inverse_1, inverse_0, early_0, early_1, prior, gain_row, gain_column, reduced_in,
+    reduced, factor, split_p, split_t, split_l, last,
+):
+    size, head = early_0.shape
+    own = place[0]
+    weight, scale = scalars[0] * scalars[0], scalars[2]
+    rows = 256
+
+    def both(inverse, early, transposed):
+        columns = slice(0, size) if transposed else slice(size, 2 * size)
+        split_p[0], split_p[1] = halves(inverse[...])
+        split_t[0], split_t[1] = halves(scale * prior[:, columns])
+        for first in range(0, size, rows):
+            here = slice(first, first + rows)
+            if transposed:
+                part = product((split_t[0, :, here], split_t[1, :, here]), (split_p[0], split_p[1]), TN)
+            else:
+                part = product((split_t[0, here], split_t[1, here]), (split_p[0], split_p[1]), NN)
+            split_l[0, here], split_l[1, here] = halves(part)
+            if first + rows > head:
+                skip = max(head - first, 0)
+                last[first + skip - head : first + rows - head, :] = part[skip:]
+        upper = (split_l[0, :head], split_l[1, :head])
+        lower = early[head:, :]
+        middle = product(halves(early[:head, :]), upper, NN)
+        last[...] -= product(halves(lower), upper, NN)
+        eye = lax.broadcasted_iota(jnp.int32, (size - head, size - head), 0) == lax.broadcasted_iota(
+            jnp.int32, (size - head, size - head), 1
+        )
+        gain_0, gain_1 = gain_row[:, :size], gain_row[:, size:]
+        factor[:, :head] = -lower * gain_0[:, :head]
+        factor[:, head:size] = jnp.where(eye, 1.0, 0.0) * gain_0[:, head:]
+        factor[:, size:] = -last[...] * gain_1
+        if transposed:
+            reduced[:, :head] = reduced_in[:, :head] + weight * middle.T * gain_column[...] * gain_0[:, :head]
+            reduced[:, head:size] = reduced_in[:, head:size]
+            middle_parts = halves(middle)
+            for first in range(0, size, rows):
+                here = slice(first, first + rows)
+                term = inverse[here, :] + product(
+                    (split_l[0, :head, here], split_l[1, :head, here]), middle_parts, TN
+                )
+                reduced[here, size:] = reduced_in[here, size:] - weight * term * gain_column[here, :] * gain_1
+        else:
+            top = weight * gain_column[:head, :]
+            reduced[:head, :head] = reduced_in[:head, :head] - top * early[:head, :] * gain_0[:, :head]
+            reduced[:head, head:size] = reduced_in[:head, head:size]
+            reduced[:head, size:] = reduced_in[:head, size:] + top * middle * gain_1
+            reduced[head:, :] = reduced_in[head:, :]
+
+    @pl.when(own == 0)
+    def _():
+        both(inverse_0, early_0, False)
+
+    @pl.when(own == 1)
+    def _():
+        both(inverse_1, early_1, True)
+
+
+def next_rows(place, scalars, inverse_1, inverse_0, early_0, early_1, prior, gain_row, gain_column, reduced):
+    size, head = early_0.shape
+    smem = pl.BlockSpec(memory_space=pltpu.SMEM)
+    vmem = pl.BlockSpec(memory_space=pltpu.VMEM)
+    return pl.pallas_call(
+        next_kernel,
+        out_shape=(
+            jax.ShapeDtypeStruct(prior.shape, F32),
+            jax.ShapeDtypeStruct((size - head, 2 * size), F32),
+        ),
+        in_specs=[smem] * 2 + [vmem] * 8,
+        out_specs=(vmem, vmem),
+        scratch_shapes=[pltpu.VMEM((2, size, size), BF16)] * 3 + [pltpu.VMEM((size - head, size), F32)],
         compiler_params=pltpu.CompilerParams(vmem_limit_bytes=48 * MIB),
-        cost_estimate=pl.CostEstimate(flops=6 * prior.size * tiles.shape[0], bytes_accessed=24 * MIB, transcendentals=0),
-        name="separator",
-    )(place, time_diag, rho, tiles, prior, schur)
+        cost_estimate=pl.CostEstimate(flops=20 * size**3, bytes_accessed=24 * MIB, transcendentals=0),
+        name="next_rows",
+    )(place, scalars, inverse_1, inverse_0, early_0, early_1, prior, gain_row, gain_column, reduced)
+
+
+def last_kernel(place, scalars, tail_0, tail_1, factor, reduced_in, reduced, split):
+    size = reduced.shape[0]
+    own = place[0]
+    weight = scalars[0] * scalars[0]
+    own_columns = pl.ds(pl.multiple_of(own * size, size), size)
+    split[0], split[1] = halves(factor[...])
+    tail = jnp.where(own == 0, tail_0[...], tail_1[...])
+    solved = halves(product(halves(tail), halves(factor[:, own_columns]), NN))
+    rows = 256
+    for first in range(0, size, rows):
+        here = slice(first, first + rows)
+        part = product((solved[0][:, here], solved[1][:, here]), (split[0], split[1]), TN)
+        reduced[here, :] = reduced_in[here, :] - weight * part
+
+
+def last_rows(place, scalars, tail_0, tail_1, factor, reduced):
+    smem = pl.BlockSpec(memory_space=pltpu.SMEM)
+    vmem = pl.BlockSpec(memory_space=pltpu.VMEM)
+    return pl.pallas_call(
+        last_kernel,
+        out_shape=jax.ShapeDtypeStruct(reduced.shape, F32),
+        in_specs=[smem] * 2 + [vmem] * 4,
+        out_specs=vmem,
+        scratch_shapes=[pltpu.VMEM((2, *factor.shape), BF16)],
+        compiler_params=pltpu.CompilerParams(vmem_limit_bytes=44 * MIB),
+        cost_estimate=pl.CostEstimate(
+            flops=6 * reduced.size * factor.shape[0], bytes_accessed=12 * MIB, transcendentals=0
+        ),
+        name="last_rows",
+    )(place, scalars, tail_0, tail_1, factor, reduced)
 
 
 def from_next(x):
@@ -334,26 +515,58 @@
     return lax.all_to_all(x, "tm", split_axis=0, concat_axis=0, tiled=True).reshape(-1, x.shape[-1])
 
 
+def from_next_core(x, core):
+    count = lax.axis_size("tm")
+    pairs = [(2 * i + core, 2 * (i - 1) + core) for i in range(1, count)]
+    return lax.ppermute(x, ("tm", "tile"), pairs)
+
+
+def across(x, core):
+    return lax.ppermute(x, "tile", [(core, 1 - core)])
+
+
+def after(x, *others):
+    return lax.optimization_barrier((x, *others))[0]
+
+
 def on_device(prior, node_gain, time_diag, rho, values, weights, steps):
     size, nodes = prior.shape
+    head = size // 2
     own = lax.axis_index("tile")
     place = own.reshape(1).astype(jnp.int32)
     interior, separator = reorder(steps[0, 0], weights[0].T, values[0])
-    next_rho = from_next(rho)
+    scalars = from_next(jnp.concatenate([rho, time_diag]))
     gain_row = node_gain.reshape(1, nodes)
     gain_column = lax.dynamic_slice_in_dim(node_gain, own * size, size).reshape(size, 1)
     interior = to_partitions(interior)
-    interior, separator = lax.optimization_barrier((interior, separator))
+    interior, separator, scalars, gain_row, gain_column = lax.optimization_barrier(
+        (interior, separator, scalars, gain_row, gain_column)
+    )
     separator = to_partitions(separator)
     block, own_inverse, own_log = invert_own(place, time_diag, interior, prior)
     other_inverse = from_other(own_inverse)
-    schur, rest_log = invert_rest(place, time_diag, other_inverse, block, prior, gain_row, gain_column)
-    incoming = from_next(schur)
-    log = jnp.where(own == 0, own_log, rest_log).reshape(1)
-    interior_logdet = (log + from_other(log)) / nodes
-    reduced, coupling = separator_rows(place, time_diag, rho, separator, prior, schur)
-    separator_block = reduced - next_rho[0] * next_rho[0] * incoming
-    return separator_block[None], coupling[None], interior_logdet
+    next_inverse_1 = from_next_core(own_inverse, 1)
+    assembled = assemble_separator(place, time_diag, after(separator, own_log), prior)
+    other_inverse = after(other_inverse, assembled)
+    reached, early, rest, head_log = invert_head(place, time_diag, other_inverse, block, prior, head)
+    next_early_0 = from_next_core(early, 0)
+    next_inverse_1 = after(next_inverse_1, head_log)
+    next_inverse_0 = across(next_inverse_1, 1)
+    tail, tail_log = invert_tail(after(rest, next_inverse_1))
+    log = jnp.where(own == 0, own_log, head_log + tail_log).reshape(1)
+    other_log = from_other(log)
+    next_tail_0 = from_next_core(tail, 0)
+    next_early_1 = across(next_early_0, 0)
+    tail = after(tail, next_early_0)
+    reduced, coupling = own_rows(place, rho, tail, early, reached, assembled, gain_row, gain_column)
+    reduced = after(reduced, other_log)
+    reduced, factor = next_rows(
+        place, scalars, next_inverse_1, next_inverse_0, next_early_0, next_early_1, prior, gain_row, gain_column, reduced
+    )
+    next_tail_1 = across(next_tail_0, 0)
+    reduced = last_rows(place, scalars, next_tail_0, next_tail_1, factor, reduced)
+    interior_logdet = (log + other_log) / nodes
+    return reduced[None], coupling[None], interior_logdet
 
 
 def solution(mesh):

time: 345 us -> 240 us (0.70)
  waiting for transfers between devices: 182 us -> 42.4 us
  Pallas kernels: 115 us -> 137 us
  starting transfers between devices: 28.3 us -> 38.9 us
  other arithmetic: 7 us -> 0.08 us
  local copies, waits for them, and re-layouts: 9.12 us -> 14.1 us
    ppermute x2 -> x1, waiting for transfers between devices: 139 us -> 31.6 us  [from_next(): return lax.ppermute(x, 'tm', [(i, i - 1) for i in range(1, count)])]
    all_to_all x2, waiting for transfers between devices: 37.9 us -> 3.32 us  [to_partitions(): lax.all_to_all(x, 'tm', split_axis=0, concat_axis=0, tiled=True)]
    pallas_call x2 -> x6, Pallas kernels: 65.5 us -> 84.6 us  [the longest x1 30.1 us: invert_head(): pl.pallas_call(head_kernel, out_shape=(shape(size, size), shape(size, hea...]
    ppermute x0 -> x6, starting transfers between devices: none -> 12.9 us  [the longest x3 7.8 us: from_next_core(): return lax.ppermute(x, ('tm', 'tile'), pairs)]
    ppermute x0 -> x6, waiting for transfers between devices: none -> 7.18 us  [the longest x3 7.17 us: from_next_core(): return lax.ppermute(x, ('tm', 'tile'), pairs)]
    broadcast_in_dim x1 -> x0, other arithmetic: 7 us -> none  [on_device(): return (separator_block[None], coupling[None], interior_logdet)]
    unnamed x18 -> x24, local copies, waits for them, and re-layouts: 8.88 us -> 13.9 us
    ppermute x2, waiting for transfers between devices: 4.7 us -> 0.28 us  [from_other(): return lax.ppermute(x, 'tile', [(0, 1), (1, 0)])]
  transfers between devices with their start and end apart: 6 -> 11, of which waited for: 4 -> 5; matrix products, arithmetic and copies ran while one was open for 0% -> 0% of each run, Pallas kernels for 4% -> 51%
where the time goes in v2:
time: 240 us; the launch traced here: 237 us
  Pallas kernels  137 us (57%)
  waiting for transfers between devices  42.4 us (18%)
  starting transfers between devices  38.9 us (16%)
  local copies, waits for them, and re-layouts  14.1 us (6%)
  between operations  4.87 us (2%)
    pallas_call x1, Pallas kernels, invert_own(): pl.pallas_call(own_kernel, out_shape=(square, square, jax.ShapeDtypeStruc...  46 us
    ppermute x1, waiting for transfers between devices, from_next(): return lax.ppermute(x, 'tm', [(i, i - 1) for i in range(1, count)])  31.6 us
    pallas_call x1, Pallas kernels, invert_head(): pl.pallas_call(head_kernel, out_shape=(shape(size, size), shape(size, hea...  30.1 us
    all_to_all x2, starting transfers between devices, to_partitions(): lax.all_to_all(x, 'tm', split_axis=0, concat_axis=0, tiled=True)  22.2 us
    pallas_call x1, Pallas kernels, invert_tail(): pl.pallas_call(tail_kernel, out_shape=(jax.ShapeDtypeStruct(rest.shape, F...  16.3 us
    unnamed x24, local copies, waits for them, and re-layouts  13.9 us
    pallas_call x1, Pallas kernels, next_rows(): pl.pallas_call(next_kernel, out_shape=(jax.ShapeDtypeStruct(prior.shape,...  13.3 us
    pallas_call x1, Pallas kernels, own_rows(): pl.pallas_call(rows_kernel, out_shape=(out, out), in_specs=[smem] * 2 + [...  11.1 us
  transfers between devices with their start and end apart: 11, of which 5 were waited for; matrix products, arithmetic and copies ran while one was open for 0% of the time, Pallas kernels for 51%

profile of v2, /device:TPU:30, one launch (start us, length us, event | category | flops | bytes accessed | tf_op | source)
XLA Modules:
  0.0 237.0 jit_solution(262827538984713593)
XLA Ops:
  0.6 6.1 %reorder.1 = (f32[64,16,768]{2,1,0:T(8,128)}, f32[64,16,768]{2,1,0:T(8,128)}) custom-call(s32[128]{0:T(128)} %bitcast.17, f32[16,128]{1,0:T(8,128)} %bitcast.16, f32[128,16,768]{2,1,0:T(8,128)} %bitcast.13), custom_call_target="tpu_custom_call" | custom-call | tf_op jit(solution)/shard_map/reorder/pallas_call | solution.py:62
  6.8 11.2 %all-to-all-start = ((f32[64,16,768]{2,1,0:T(8,128)}), f32[64,16,768]{2,1,0:T(8,128)S(1)}, u32[]{:S(2)}, u32[]{:S(2)}) async-start(f32[64,16,768]{2,1,0:T(8,128)} %get-tuple-element.29), calls=%async_computation | async-start | bytes 6291456 | tf_op jit(solution)/shard_map/all_to_all | solution.py:515
  18.1 2.8 %collective-permute-start = (f32[4]{0:T(128)S(1)}, f32[4]{0:T(128)S(1)}, u32[]{:S(2)}, u32[]{:S(2)}) collective-permute-start(f32[4]{0:T(128)S(1)} %pad_maximum_fusion), channel_id=1, source_target_pairs={{2,0},{4,2},{6,4},{8,6},{10,8},{12,10},{14,12},{16,14},{18,16},{20... | collective-permute-start | bytes 56 | tf_op jit(solution)/shard_map/ppermute | solution.py:507
  21.0 31.6 %collective-permute-done.scalars = f32[4]{0:T(128)S(1)} collective-permute-done((f32[4]{0:T(128)S(1)}, f32[4]{0:T(128)S(1)}, u32[]{:S(2)}, u32[]{:S(2)}) %collective-permute-start) | collective-permute-done | bytes 48 | tf_op jit(solution)/shard_map/ppermute | solution.py:507
  52.6 3.3 %all-to-all-done = f32[64,16,768]{2,1,0:T(8,128)S(1)} async-done(((f32[64,16,768]{2,1,0:T(8,128)}), f32[64,16,768]{2,1,0:T(8,128)S(1)}, u32[]{:S(2)}, u32[]{:S(2)}) %all-to-all-start) | async-done | bytes 3145760 | tf_op jit(solution)/shard_map/all_to_all | solution.py:515
  56.0 1.7 copy-done.10
  57.6 11.0 %all-to-all-start.1 = ((f32[64,16,768]{2,1,0:T(8,128)}), f32[64,16,768]{2,1,0:T(8,128)S(1)}, u32[]{:S(2)}, u32[]{:S(2)}) async-start(f32[64,16,768]{2,1,0:T(8,128)} %get-tuple-element.34), calls=%async_computation.1 | async-start | bytes 6291456 | tf_op jit(solution)/shard_map/all_to_all | solution.py:515
  68.6 46.0 %invert_own.1 = (f32[768,768]{1,0:T(8,128)S(1)}, f32[768,768]{1,0:T(8,128)}, f32[1,1]{1,0:T(1,128)}) custom-call(s32[1]{0:T(128)} %bitcast.place, f32[2]{0:T(128)S(1)} %copy-done.2, f32[1024,768]{1,0:T(8,128)} %bitcast.15, f32[768,1536]{1,0:T(8,128)} %prior.7), custom_call_target="tpu_custom_call" | custom-call | flops 18119393280 | bytes 16777216 | tf_op jit(solution)/shard_map/invert_own/pallas_call | solution.py:225
  116.1 2.6 %collective-permute-start.2 = (f32[768,768]{1,0:T(8,128)}, f32[768,768]{1,0:T(8,128)}, u32[]{:S(2)}, u32[]{:S(2)}) collective-permute-start(f32[768,768]{1,0:T(8,128)} %get-tuple-element.33), channel_id=1, source_target_pairs={{3,1},{5,3},{7,5},{9,7},{11,9},{13,11},{15,13},{17,15},{19,17},{21... | collective-permute-start | bytes 7077896 | tf_op jit(solution)/shard_map/ppermute | solution.py:521
  118.7 2.3 copy-done.1
  121.1 4.8 %assemble_separator.1.assembled = f32[768,1536]{1,0:T(8,128)S(1)} custom-call(s32[1]{0:T(128)} %bitcast.place, f32[2]{0:T(128)S(1)} %copy-done.2, f32[1024,768]{1,0:T(8,128)S(1)} %bitcast.12, f32[768,1536]{1,0:T(8,128)S(1)} %copy-done.1), custom_call_target="tpu_custom_call" | custom-call | flops 7247757312 | bytes 14680064 | tf_op jit(solution)/shard_map/assemble_separator/pallas_call | solution.py:336
  125.9 2.2 copy-done.4
  128.1 30.1 %invert_head.1 = (f32[768,768]{1,0:T(8,128)S(1)}, f32[768,384]{1,0:T(8,128)S(1)}, f32[384,384]{1,0:T(8,128)S(1)}, f32[1,1]{1,0:T(1,128)}) custom-call(s32[1]{0:T(128)} %bitcast.place, f32[2]{0:T(128)S(1)} %copy-done.2, f32[768,768]{1,0:T(8,128)} %collective-permute-done.1.other_inverse, f32[768,768]{1,0:T(8,128)S(1)} %copy-done.9, f32[768,1536]{1,0:T(8,128)} %prior.7), custom_call_target="tpu_custom_call" | custom-call | flops 36238786560 | bytes 16777216 | tf_op jit(solution)/shard_map/invert_head/pallas_call | solution.py:273
  159.4 2.8 %collective-permute-start.6 = (f32[768,384]{1,0:T(8,128)S(1)}, f32[768,384]{1,0:T(8,128)}, u32[]{:S(2)}, u32[]{:S(2)}) collective-permute-start(f32[768,384]{1,0:T(8,128)S(1)} %get-tuple-element.44.early), channel_id=1, source_target_pairs={{2,0},{4,2},{6,4},{8,6},{10,8},{12,10},{14,12},{16,14},{18,16},{20... | collective-permute-start | bytes 3538952 | tf_op jit(solution)/shard_map/ppermute | solution.py:521
  162.2 16.3 %invert_tail.1 = (f32[384,384]{1,0:T(8,128)S(1)}, f32[1,1]{1,0:T(1,128)}) custom-call(f32[384,384]{1,0:T(8,128)S(1)} %get-tuple-element.42.rest), custom_call_target="tpu_custom_call" | custom-call | flops 11324620800 | bytes 4194304 | tf_op jit(solution)/shard_map/invert_tail/pallas_call | solution.py:306
  178.6 2.5 %collective-permute-start.3 = (f32[384,384]{1,0:T(8,128)S(1)}, f32[384,384]{1,0:T(8,128)S(1)}, u32[]{:S(2)}, u32[]{:S(2)}) collective-permute-start(f32[384,384]{1,0:T(8,128)S(1)} %get-tuple-element.47.tail), channel_id=1, source_target_pairs={{2,0},{4,2},{6,4},{8,6},{10,8},{12,10},{14,12},{16,14},{18,16},{20... | collective-permute-start | bytes 1769480 | tf_op jit(solution)/shard_map/ppermute | solution.py:521
  181.9 2.3 collective-permute-start.7
  188.2 6.3 %collective-permute-done.3.tail_0 = f32[384,384]{1,0:T(8,128)S(1)} collective-permute-done((f32[384,384]{1,0:T(8,128)S(1)}, f32[384,384]{1,0:T(8,128)S(1)}, u32[]{:S(2)}, u32[]{:S(2)}) %collective-permute-start.3) | collective-permute-done | bytes 589856 | tf_op jit(solution)/shard_map/ppermute | solution.py:521
  196.1 1.7 copy-done.7
  197.7 11.1 %own_rows.1 = (f32[768,1536]{1,0:T(8,128)S(1)}, f32[768,1536]{1,0:T(8,128)}) custom-call(s32[1]{0:T(128)} %bitcast.place, f32[2]{0:T(128)S(1)} %copy-done.3, f32[384,384]{1,0:T(8,128)S(1)} %get-tuple-element.47.tail, f32[768,384]{1,0:T(8,128)S(1)} %get-tuple-element.44.early, f32[768,768]{1,0:T(8,128)S(1)} %copy-done.7, f32[768,1536]{1,0:T(8,128)} %copy-done.4, ...), custom_call_target="tpu_custom_call" | custom-call | flops 9059696640 | bytes 25165824 | tf_op jit(solution)/shard_map/own_rows/pallas_call | solution.py:382
  208.9 2.2 copy-done.5
  211.1 13.3 %next_rows.1 = (f32[768,1536]{1,0:T(8,128)}, f32[384,1536]{1,0:T(8,128)S(1)}) custom-call(s32[1]{0:T(128)} %bitcast.place, f32[4]{0:T(128)S(1)} %collective-permute-done.scalars, f32[768,768]{1,0:T(8,128)} %collective-permute-done.2.inverse_1, f32[768,768]{1,0:T(8,128)} %collective-permute-done.5.inverse_0, f32[768,384]{1,0:T(8,128)} %collective-permute-done.6.early_0, ...), custom_call_target="tpu_custom_call" | custom-call | flops 9059696640 | bytes 25165824 | tf_op jit(solution)/shard_map/next_rows/pallas_call | solution.py:458
  224.3 2.3 copy-done
  226.7 8.9 %last_rows.1 = f32[768,1536]{1,0:T(8,128)} custom-call(s32[1]{0:T(128)} %bitcast.place, f32[4]{0:T(128)S(1)} %collective-permute-done.scalars, f32[384,384]{1,0:T(8,128)S(1)} %collective-permute-done.3.tail_0, f32[384,384]{1,0:T(8,128)S(1)} %collective-permute-done.4.tail_1, f32[384,1536]{1,0:T(8,128)S(1)} %get-tuple-element.52.factor, f32[768,1536]{1,0:T(8,128)S(1)} %copy-done), custom_call_target="tpu_custom_call" | custom-call | flops 2717908992 | bytes 12582912 | tf_op jit(solution)/shard_map/last_rows/pallas_call | solution.py:491
  (35 shorter events, 6.7 us)
Async XLA Ops:
  6.8 11.3 %copy-start.2 = (f32[2]{0:T(128)S(1)}, f32[2]{0:T(128)}, u32[]{:S(2)}) copy-start(f32[2]{0:T(128)} %time_diag.5) | copy-start | bytes 28
  6.8 11.3 %copy-start.3 = (f32[2]{0:T(128)S(1)}, f32[2]{0:T(128)}, u32[]{:S(2)}) copy-start(f32[2]{0:T(128)} %rho.1) | copy-start | bytes 28
  6.8 14.1 %copy-start.11 = (f32[1536]{0:T(1024)S(1)}, f32[1536]{0:T(1024)}, u32[]{:S(2)}) copy-start(f32[1536]{0:T(1024)} %param.8) | copy-start | bytes 18436
  6.8 49.2 %all-to-all-start = ((f32[64,16,768]{2,1,0:T(8,128)}), f32[64,16,768]{2,1,0:T(8,128)S(1)}, u32[]{:S(2)}, u32[]{:S(2)}) async-start(f32[64,16,768]{2,1,0:T(8,128)} %get-tuple-element.29), calls=%async_computation | async-start | bytes 6291456 | tf_op jit(solution)/shard_map/all_to_all | solution.py:515
  18.1 34.5 %collective-permute-start = (f32[4]{0:T(128)S(1)}, f32[4]{0:T(128)S(1)}, u32[]{:S(2)}, u32[]{:S(2)}) collective-permute-start(f32[4]{0:T(128)S(1)} %pad_maximum_fusion), channel_id=1, source_target_pairs={{2,0},{4,2},{6,4},{8,6},{10,8},{12,10},{14,12},{16,14},{18,16},{20... | collective-permute-start | bytes 56 | tf_op jit(solution)/shard_map/ppermute | solution.py:507
  56.0 1.7 copy-start.10
  57.6 61.1 %all-to-all-start.1 = ((f32[64,16,768]{2,1,0:T(8,128)}), f32[64,16,768]{2,1,0:T(8,128)S(1)}, u32[]{:S(2)}, u32[]{:S(2)}) async-start(f32[64,16,768]{2,1,0:T(8,128)} %get-tuple-element.34), calls=%async_computation.1 | async-start | bytes 6291456 | tf_op jit(solution)/shard_map/all_to_all | solution.py:515
  114.6 1.5 copy-start.8
  116.1 11.9 %collective-permute-start.1 = (f32[768,768]{1,0:T(8,128)}, f32[768,768]{1,0:T(8,128)}, u32[]{:S(2)}, u32[]{:S(2)}) collective-permute-start(f32[768,768]{1,0:T(8,128)} %get-tuple-element.33), channel_id=1, source_target_pairs={{0,1},{1,0},{2,3},{3,2},{4,5},{5,4},{6,7},{7,6},{8,9},{9,8},{10,11... | collective-permute-start | bytes 7077896 | tf_op jit(solution)/shard_map/ppermute | solution.py:511
  116.1 42.0 %collective-permute-start.2 = (f32[768,768]{1,0:T(8,128)}, f32[768,768]{1,0:T(8,128)}, u32[]{:S(2)}, u32[]{:S(2)}) collective-permute-start(f32[768,768]{1,0:T(8,128)} %get-tuple-element.33), channel_id=1, source_target_pairs={{3,1},{5,3},{7,5},{9,7},{11,9},{13,11},{15,13},{17,15},{19,17},{21... | collective-permute-start | bytes 7077896 | tf_op jit(solution)/shard_map/ppermute | solution.py:521
  118.7 2.3 copy-start.1
  121.1 7.0 %copy-start.9 = (f32[768,768]{1,0:T(8,128)S(1)}, f32[768,768]{1,0:T(8,128)}, u32[]{:S(2)}) copy-start(f32[768,768]{1,0:T(8,128)} %copy-done.8) | copy-start | bytes 7077892
  125.9 2.2 copy-start.4
  158.1 20.4 %copy-start.6 = (f32[768,768]{1,0:T(8,128)}, f32[768,768]{1,0:T(8,128)S(1)}, u32[]{:S(2)}) copy-start(f32[768,768]{1,0:T(8,128)S(1)} %get-tuple-element.48.reached) | copy-start | bytes 7077892
  158.1 52.9 %collective-permute-start.5 = (f32[768,768]{1,0:T(8,128)}, f32[768,768]{1,0:T(8,128)}, u32[]{:S(2)}, u32[]{:S(2)}) collective-permute-start(f32[768,768]{1,0:T(8,128)} %collective-permute-done.2.inverse_1), channel_id=1, source_target_pairs={{1,0},{3,2},{5,4},{7,6},{9,8},{11,10},{13,12},{15,14},{17,16},{19,... | collective-permute-start | bytes 7077896 | tf_op jit(solution)/shard_map/ppermute | solution.py:525
  159.4 22.4 %collective-permute-start.6 = (f32[768,384]{1,0:T(8,128)S(1)}, f32[768,384]{1,0:T(8,128)}, u32[]{:S(2)}, u32[]{:S(2)}) collective-permute-start(f32[768,384]{1,0:T(8,128)S(1)} %get-tuple-element.44.early), channel_id=1, source_target_pairs={{2,0},{4,2},{6,4},{8,6},{10,8},{12,10},{14,12},{16,14},{18,16},{20... | collective-permute-start | bytes 3538952 | tf_op jit(solution)/shard_map/ppermute | solution.py:521
  178.6 16.0 %collective-permute-start.3 = (f32[384,384]{1,0:T(8,128)S(1)}, f32[384,384]{1,0:T(8,128)S(1)}, u32[]{:S(2)}, u32[]{:S(2)}) collective-permute-start(f32[384,384]{1,0:T(8,128)S(1)} %get-tuple-element.47.tail), channel_id=1, source_target_pairs={{2,0},{4,2},{6,4},{8,6},{10,8},{12,10},{14,12},{16,14},{18,16},{20... | collective-permute-start | bytes 1769480 | tf_op jit(solution)/shard_map/ppermute | solution.py:521
  181.9 29.2 %collective-permute-start.7 = (f32[768,384]{1,0:T(8,128)}, f32[768,384]{1,0:T(8,128)}, u32[]{:S(2)}, u32[]{:S(2)}) collective-permute-start(f32[768,384]{1,0:T(8,128)} %collective-permute-done.6.early_0), channel_id=1, source_target_pairs={{0,1},{2,3},{4,5},{6,7},{8,9},{10,11},{12,13},{14,15},{16,17},{18,... | collective-permute-start | bytes 3538952 | tf_op jit(solution)/shard_map/ppermute | solution.py:525
  186.3 1.2 collective-permute-start.8
  194.5 29.8 %collective-permute-start.4 = (f32[384,384]{1,0:T(8,128)S(1)}, f32[384,384]{1,0:T(8,128)S(1)}, u32[]{:S(2)}, u32[]{:S(2)}) collective-permute-start(f32[384,384]{1,0:T(8,128)S(1)} %collective-permute-done.3.tail_0), channel_id=1, source_target_pairs={{0,1},{2,3},{4,5},{6,7},{8,9},{10,11},{12,13},{14,15},{16,17},{18,... | collective-permute-start | bytes 1769480 | tf_op jit(solution)/shard_map/ppermute | solution.py:525
  196.1 1.7 copy-start.7
  208.9 2.2 copy-start.5
  224.3 2.3 copy-start
